TPU v7x, 128 devices: a whole 4x4x4 slice. The times are simulated.
128 devices in a mesh: dp: 32 (over x, z, core), ep: 4 (over y).
Axes of the slice: x: 4, y: 4, z: 4, core: 2. Of those that a mesh axis runs over, the one named last changes fastest.
Arguments:
- kv_cache: bfloat16 [8192, 36864], P(('dp', 'ep')), may hold values from -6 to 6
- slot_fill: int32 [8192], P(('dp', 'ep')), may hold values from 0 to 64, as said below
- slot_request: int32 [8192], P(('dp', 'ep')), may hold values from 0 to 3
- moved_slot: int32 [2048], P(('dp', 'ep')), may hold values from 0 to 63, as said below
- moved_target: int32 [2048, 1], P(('dp', 'ep')), may hold values from 0 to 31; in each aligned block of 16 rows (0 to 15, 16 to 31, ...) no two rows name the same one
- queries: bfloat16 [2, 512, 73728], P(None, ('dp', 'ep')), may hold values from -48 to 48
- new_kv: bfloat16 [2, 512, 576], P(None, ('dp', 'ep')), may hold values from -8 to 8
- expert_input: bfloat16 [2, 1024, 3584], P(None, ('dp', 'ep')), may hold values from -6 to 6
- expert_ids: int32 [2, 1024, 8], P(None, ('dp', 'ep')), may hold values from 0 to 63, all different within a row; in each aligned block of 8 rows (0 to 7, 8 to 15, ..., all dimensions but the last counted through in order) at most 2 rows name the same one
- gate_weights: float32 [2, 1024, 8], P(None, ('dp', 'ep')), may hold values from 0.1 to 1
- w_gate: bfloat16 [64, 3584, 1024], P('dp', None, 'ep'), may hold values from -0.09375 to 0.09375
- w_up: bfloat16 [64, 3584, 1024], P('dp', None, 'ep'), may hold values from -0.09375 to 0.09375
- down_weight: bfloat16 [64, 1024, 3584], P('dp', 'ep'), may hold values from -0.1875 to 0.1875
Outputs:
- guest_pages: bfloat16 [4096, 36864], P(('dp', 'ep'))
- attention_out: bfloat16 [2, 512, 65536], P(None, ('dp', 'ep'))
- expert_out: bfloat16 [2, 1024, 3584], P(None, ('dp', 'ep'))
Inputs may be any that keep to these rules, and one draw needn't show every extreme that they name: `slot_fill`: valid tokens from the start of the slot; 0 marks a free slot. `slot_request`: the request's index among the 4 requests of the slot's own device. `moved_slot`: the 16 entries of one device name distinct slots of that device. `moved_target`: no dp index is named by more than 1 of the 16 entries of one device. `expert_ids`: the 8 ids of a token are distinct, and in a step no expert is named by more than 2 of the 8 tokens of one device.
All inputs are finite; a program needn't handle non-finite values.
Results may differ from a plain program's by a relative error of at most 0.0065.
Values may be sent and summed in bfloat16 or wider, within the bound.
No kernel may reach another device: no remote copies, remote signals or barrier semaphores. Data moves between devices by JAX's collectives and lax.ppermute only.
A program may use at most 192 MiB of HBM per device.

v0:
```python
import collections
import functools

import jax
import jax.numpy as jnp
from jax import lax
from jax.experimental import pallas as pl
from jax.experimental.pallas import tpu as pltpu
from jax.sharding import PartitionSpec as P

D = 3584
H = 128
LAT = 512
PAGE = 64
TOP = 8
STEPS = 2
REQ = 4
SLOTS = 64
TOK = 8
KVW = 576
FFD = 256
EXPERTS = 64
CAP = 2
DQ = D // 4
XW = D + 128
KPAD = 640
ROWS = STEPS * REQ * H
MASKED = -1e30
SCORE_SCALE = 192.0 ** (-0.5)
ORDER = (0, 1, 3, 2)
VMEM = 56 * 1024 * 1024


def params(**more):
    return pltpu.CompilerParams(vmem_limit_bytes=VMEM, **more)


def iota(shape, dim):
    return lax.broadcasted_iota(jnp.int32, shape, dim)


PIECES_A = tuple((k, other) for k in (0, 1, 3) for other in (0, 1))
PIECES_B = ((2, 0), (2, 1))


def inner_kernel(kinds, parts, place_ref, *refs):
    n = len(kinds)
    pieces, (wg_ref, wu_ref, *before, o_ref, xs_ref) = refs[: n * parts], refs[n * parts :]
    skip = before[0].shape[1] if before else 0
    for earlier in before:
        o_ref[:, :skip] = earlier[...]
    base, px, pz, pc, py = (place_ref[i] for i in range(5))
    row = iota((256, 128), 0)
    col = iota((256, 128), 1)
    pick = (iota((128, 128), 0) == base + iota((128, 128), 1) // 64).astype(jnp.bfloat16)
    same = (row % 16) // 8 == (col % 4) // 2
    same = same & (((py - (row % 64) // 16) & 3) == (col % 16) // 4)
    wanted = (col % 2 + 1).astype(jnp.float32)
    here = []
    for other in range(2):
        at = jnp.where((pc ^ other) == 0, px, pz)
        here.append(same & (((at - row // 64) & 3) == (col % 64) // 16))
    for i, (_, other) in enumerate(kinds):
        x = jnp.concatenate([part[...] for part in pieces[i * parts : (i + 1) * parts]], axis=0)
        code = jnp.dot(x[:, D:], pick, preferred_element_type=jnp.float32)
        chosen = jnp.where(here[other] & (code == wanted), 1.0, 0.0).astype(jnp.bfloat16)
        sel = lax.dot_general(
            chosen, x[:, :D], (((0,), (0,)), ((), ())), preferred_element_type=jnp.float32
        ).astype(jnp.bfloat16)
        xs_ref[0, 64 * i : 64 * i + 64] = sel[:64]
        xs_ref[1, 64 * i : 64 * i + 64] = sel[64:]
    for e in range(2):
        rows_in = xs_ref[e]
        gate = jnp.dot(rows_in, wg_ref[e], preferred_element_type=jnp.float32)
        up = jnp.dot(rows_in, wu_ref[e], preferred_element_type=jnp.float32)
        o_ref[e, skip:] = (gate / (1.0 + jnp.exp(-gate)) * up).astype(jnp.bfloat16)


def inner_of(kinds, place, pieces, w_gate, w_up, *before):
    n = len(kinds)
    rows = 64 * n
    skip = before[0].shape[1] if before else 0
    return pl.pallas_call(
        functools.partial(inner_kernel, kinds, len(pieces) // n),
        in_specs=[pl.BlockSpec(memory_space=pltpu.SMEM)]
        + [pl.BlockSpec(memory_space=pltpu.VMEM)] * (len(pieces) + 2 + len(before)),
        out_specs=pl.BlockSpec(memory_space=pltpu.VMEM),
        out_shape=jax.ShapeDtypeStruct((2, skip + rows, FFD), jnp.bfloat16),
        scratch_shapes=[pltpu.VMEM((2, rows, D), jnp.bfloat16)],
        compiler_params=params(),
        cost_estimate=pl.CostEstimate(
            flops=1_000_000_000 * n,
            bytes_accessed=7_500_000 + 2_000_000 * n,
            transcendentals=300_000,
        ),
    )(place, *pieces, w_gate, w_up, *before)


def down_kernel(place_ref, *refs):
    inner_a, inner_b, weights = refs[:4], refs[4:8], refs[8:13]
    o_ref, part_ref, held_ref = refs[13:]
    px, pz, pc = (place_ref[i] for i in range(1, 4))
    for inner, at in ((inner_a, 0), (inner_b, 64 * len(PIECES_A))):
        rows = inner[0].shape[1]
        for e in range(2):
            total = None
            parts = [weights[i][e] for i in range(3)] + [weights[3 + e][0]]
            for part, weight in zip(inner, parts):
                term = jnp.dot(part[e], weight, preferred_element_type=jnp.float32)
                total = term if total is None else total + term
            part_ref[e, at : at + rows] = total.astype(jnp.bfloat16)
    out = iota((256, 128), 0)
    col = iota((256, 128), 1)
    spot = 2 * (col // 64) + col % 2
    for other in range(2):
        step = pc ^ other
        put = (out // 8 == (col % 64) // 2) & (out % 8 == spot + 4 * step)
        put = put.astype(jnp.bfloat16)
        near = jnp.where(step == 0, 32, 8)
        far = 40 - near
        for i, (k, whose) in enumerate(PIECES_A + PIECES_B):
            if whose != other:
                continue
            rows = slice(64 * i, 64 * i + 64)
            part = jnp.concatenate([part_ref[0, rows], part_ref[1, rows]], axis=0)
            placed = jnp.dot(put, part, preferred_element_type=jnp.float32).reshape(32, 8, DQ)
            start = ((jnp.where(step == 0, pz, px) - k) & 3) * far
            for dev in range(32):
                to = start + near * (dev // 8) + 4 * (dev % 2) + (dev % 8) // 2
                if other:
                    o_ref[to] = (held_ref[to] + placed[dev]).astype(jnp.bfloat16)
                else:
                    held_ref[to] = placed[dev]


def down_of(place, inner_a, inner_b, weights):
    rows = inner_a[0].shape[1] + inner_b[0].shape[1]
    return pl.pallas_call(
        down_kernel,
        in_specs=[pl.BlockSpec(memory_space=pltpu.SMEM)] + [pl.BlockSpec(memory_space=pltpu.VMEM)] * 13,
        out_specs=pl.BlockSpec(memory_space=pltpu.VMEM),
        out_shape=jax.ShapeDtypeStruct((128, 8, DQ), jnp.bfloat16),
        scratch_shapes=[
            pltpu.VMEM((2, rows, DQ), jnp.bfloat16),
            pltpu.VMEM((128, 8, DQ), jnp.float32),
        ],
        compiler_params=params(),
        cost_estimate=pl.CostEstimate(
            flops=3_000_000_000, bytes_accessed=8_000_000, transcendentals=0
        ),
    )(place, *inner_a, *inner_b, *weights)


def combine_kernel(mix_ref, ret_ref, o_ref):
    mix = mix_ref[...]
    high = mix.astype(jnp.bfloat16)
    rest = mix - high.astype(jnp.float32)
    mid = rest.astype(jnp.bfloat16)
    low = (rest - mid.astype(jnp.float32)).astype(jnp.bfloat16)
    tokens = mix.shape[0]
    for q in range(4):
        rows = ret_ref[:, q].astype(jnp.float32).reshape(-1, DQ).astype(jnp.bfloat16)
        total = jnp.dot(high, rows, preferred_element_type=jnp.float32)
        total = total + jnp.dot(mid, rows, preferred_element_type=jnp.float32)
        total = total + jnp.dot(low, rows, preferred_element_type=jnp.float32)
        total = total.astype(jnp.bfloat16)
        for s in range(STEPS):
            o_ref[s, :, q * DQ : (q + 1) * DQ] = total[s * TOK : (s + 1) * TOK]


def combine(mix, returned):
    return pl.pallas_call(
        combine_kernel,
        in_specs=[pl.BlockSpec(memory_space=pltpu.VMEM)] * 2,
        out_specs=pl.BlockSpec(memory_space=pltpu.VMEM),
        out_shape=jax.ShapeDtypeStruct((STEPS, TOK, D), jnp.bfloat16),
        compiler_params=params(),
    )(mix, returned.reshape(-1, 4, 8, DQ))


def experts(expert_input, expert_ids, gate_weights, w_gate, w_up, down_weight, hooks, paged, others):
    group = lax.axis_index("dp")
    rank = lax.axis_index("ep")
    ranks = lax.axis_size("ep")
    groups = lax.axis_size("dp")

    hits = expert_ids[..., None] == jnp.arange(EXPERTS, dtype=jnp.int32)
    member = jnp.any(hits, axis=2)
    counted = member.astype(jnp.int32)
    place = jnp.cumsum(counted, axis=1) - counted
    code = jnp.where(member, place + 1, 0).astype(jnp.bfloat16).reshape(STEPS * TOK, EXPERTS)
    code = jnp.pad(code, ((0, 0), (0, XW - D - EXPERTS)))
    sent = jnp.concatenate([expert_input.reshape(STEPS * TOK, D), code], axis=1)

    def over_ep(array, k):
        return lax.ppermute(array, "ep", [(i, (i + k) % ranks) for i in range(ranks)])

    def over_dp(array, move):
        pairs = []
        for i in range(groups):
            x, z, c = move(i // 8, i // 2 % 4, i % 2)
            pairs.append((i, x % 4 * 8 + z % 4 * 2 + c))
        return lax.ppermute(array, "dp", pairs)

    def sibling(array):
        return over_dp(array, lambda x, z, c: (x, z, 1 - c))

    def first_axis(array, k):
        return over_dp(array, lambda x, z, c: (x + k * (1 - c), z + k * c, c))

    def second_axis(array, k):
        return over_dp(array, lambda x, z, c: (x + k * c, z + k * (1 - c), c))

    def spread(array, move):
        return {k: move(array, k) if k else array for k in ORDER}

    def line(parts):
        return jnp.concatenate([parts[k] for k in range(4)], axis=0)

    def columns(k):
        start = lax.rem(rank + k, ranks) * DQ
        return lax.dynamic_slice_in_dim(down_weight, start, DQ, axis=2)

    def mixing(ids, gates):
        hits = ids[..., None] == jnp.arange(EXPERTS, dtype=jnp.int32)
        gates = jnp.sum(jnp.where(hits, gates[..., None], 0.0), axis=2)
        same = jnp.arange(STEPS)[:, None] == jnp.arange(STEPS)[None, :]
        at_place = place[..., None] == jnp.arange(CAP, dtype=jnp.int32)
        return (
            gates.reshape(STEPS, TOK, groups, 1, 2, 1)
            * same[:, None, None, :, None, None].astype(jnp.float32)
            * at_place.reshape(STEPS, TOK, groups, 1, 2, CAP).astype(jnp.float32)
        ).reshape(STEPS * TOK, EXPERTS * STEPS * CAP)

    core = group % 2
    step0, step1 = sent[:TOK], sent[TOK:]
    there = sibling(jnp.where(core == 0, step1, step0))
    chip = jnp.where(
        core == 0,
        jnp.concatenate([step0, there], axis=0),
        jnp.concatenate([there, step1], axis=0),
    )
    column = line(spread(chip, over_ep))
    quarters = [columns(k) for k in range(4)]
    parts = (quarters[2][:1], quarters[2][1:])
    column, others, expert_ids, gate_weights, quarters, parts = lax.optimization_barrier(
        (column, others, expert_ids, gate_weights, quarters, parts)
    )
    where = jnp.stack([2 * group, group // 8, group // 2 % 4, core, rank]).astype(jnp.int32)
    ready = hooks.operands(*others)
    mix = mixing(expert_ids, gate_weights)
    opposite = [over_ep(parts[0], 2)]
    plane = line(spread(column, first_axis))
    plane, paged, mix, where, ready, quarters, opposite = lax.optimization_barrier(
        (plane, paged, mix, where, ready, quarters, opposite)
    )
    weights = {0: quarters[0], 1: over_ep(quarters[1], 1), 3: over_ep(quarters[3], 3)}
    pieces = {1: second_axis(plane, 1), 3: second_axis(plane, 3)}
    own_a = inner_of(PIECES_A[:2], where, [plane, sibling(plane)], w_gate, w_up)
    leaving = hooks.leaving(*paged)
    pieces, own_a, weights, rest, leaving = lax.optimization_barrier(
        (pieces, own_a, weights, parts[1], leaving)
    )
    opposite.append(over_ep(rest, 2))
    early = [p for k in (1, 3) for p in (pieces[k], sibling(pieces[k]))]
    last = [second_axis(pieces[1][:128], 1), second_axis(pieces[3][128:], 3)]

    own_a = inner_of(PIECES_A[2:], where, early, w_gate, w_up, own_a)
    inner_a = [over_ep(own_a, k) if k else own_a for k in ORDER]
    last, _, opposite, leaving = lax.optimization_barrier((last, own_a, opposite, leaving))
    moved = lax.all_to_all(leaving, "dp", split_axis=0, concat_axis=0, tiled=True)
    guests = moved.reshape(groups, -1)
    last = last + [sibling(part) for part in last]
    own_b = inner_of(PIECES_B, where, last, w_gate, w_up)
    inner_b = [over_ep(own_b, k) if k else own_b for k in ORDER]
    produced = down_of(where, inner_a, inner_b, [weights[k] for k in ORDER[:3]] + opposite)
    returned = lax.all_to_all(produced, ("dp", "ep"), split_axis=0, concat_axis=0, tiled=True)
    return combine(mix, returned), guests, ready


def attention_kernel(kv_ref, qe_ref, qo_ref, fresh_ref, fill_ref, owner_ref, o_ref,
                     s_ref, sf_ref, top_ref, total_ref, even_ref, odd_ref, w_ref):
    nt = (((1,), (1,)), ((), ()))
    pairs = STEPS * REQ
    wide = 4 * SLOTS
    fill = fill_ref[...]
    owner = owner_ref[...]
    inside = iota((1, wide), 1) // SLOTS

    def keys(j, odd):
        pieces = []
        for i in range(4):
            at = pl.multiple_of((4 * j + i) * 1152 + 512 * odd, 128)
            pieces.append(kv_ref[:, pl.ds(at, KPAD)])
        return jnp.concatenate(pieces, axis=0)

    def allowed(j, odd):
        return (8 * j + 2 * inside + odd) < fill

    lane = iota((H, 128), 1)
    for p in range(pairs):
        s, r = p // REQ, p % REQ
        sc = lax.dot_general(qe_ref[p * H : (p + 1) * H], fresh_ref[...], nt,
                             preferred_element_type=jnp.float32)
        ok = (lane % REQ == r) & (lane // REQ <= s)
        sc = jnp.where(ok, sc, MASKED)
        sf_ref[p * H : (p + 1) * H] = sc
        top_ref[p * H : (p + 1) * H] = jnp.concatenate([sc, sc], axis=1)

    def first(j, carry):
        for odd in range(2):
            k = keys(j, odd)
            ok = allowed(j, odd)
            q_ref = qo_ref if odd else qe_ref
            s_ref[2 * j + odd] = lax.dot_general(q_ref[...], k, nt, preferred_element_type=jnp.float32)
            for p in range(pairs):
                rows = slice(p * H, (p + 1) * H)
                sc = jnp.where(ok & (owner == p % REQ), s_ref[2 * j + odd, rows], MASKED)
                top_ref[rows] = jnp.maximum(top_ref[rows], sc)
        return carry

    lax.fori_loop(0, PAGE // 8, first, 0)

    for p in range(pairs):
        rows = slice(p * H, (p + 1) * H)
        top = jnp.max(top_ref[rows], axis=1, keepdims=True) * SCORE_SCALE
        top_ref[rows] = jnp.broadcast_to(top, (H, wide))
        w = jnp.exp(sf_ref[rows] * SCORE_SCALE - top)
        total_ref[rows] = jnp.concatenate([w, jnp.zeros_like(w)], axis=1)
        even_ref[rows] = jnp.dot(w.astype(jnp.bfloat16), fresh_ref[:, :LAT],
                                 preferred_element_type=jnp.float32)
        odd_ref[rows] = jnp.zeros((H, KPAD), jnp.float32)

    def second(jj, carry):
        for odd in range(2):
            for half in range(2):
                j = 2 * jj + half
                ok = allowed(j, odd)
                for p in range(pairs):
                    rows = slice(p * H, (p + 1) * H)
                    w = jnp.exp(s_ref[2 * j + odd, rows] * SCORE_SCALE - top_ref[rows])
                    w = jnp.where(ok & (owner == p % REQ), w, 0.0)
                    total_ref[rows] += w
                    w_ref[rows, half * wide : (half + 1) * wide] = w.astype(jnp.bfloat16)
            k = jnp.concatenate([keys(2 * jj, odd), keys(2 * jj + 1, odd)], axis=0)
            if odd:
                odd_ref[...] += jnp.dot(w_ref[...], k, preferred_element_type=jnp.float32)
            else:
                even_ref[...] += jnp.dot(w_ref[...], k[:, :LAT], preferred_element_type=jnp.float32)
        return carry

    lax.fori_loop(0, PAGE // 16, second, 0)

    for p in range(pairs):
        rows = slice(p * H, (p + 1) * H)
        total = jnp.sum(total_ref[rows], axis=1, keepdims=True)
        value = even_ref[rows] + odd_ref[rows, 64 : 64 + LAT]
        o_ref[rows] = (value / total).astype(jnp.bfloat16)


def attention_operands(slot_fill, slot_request, queries, new_kv):
    q = queries.reshape(ROWS, KVW)
    q_even = jnp.pad(q, ((0, 0), (0, KPAD - KVW)))
    q_odd = jnp.pad(q, ((0, 0), (KPAD - KVW, 0)))
    fresh = jnp.pad(new_kv.reshape(STEPS * REQ, KVW), ((0, 128 - STEPS * REQ), (0, KPAD - KVW)))
    fill = jnp.tile(slot_fill, 4).reshape(1, 4 * SLOTS)
    owner = jnp.tile(slot_request, 4).reshape(1, 4 * SLOTS)
    return q_even, q_odd, fresh, fill, owner


def attention(kv_cache, operands):
    wide = 4 * SLOTS
    out = pl.pallas_call(
        attention_kernel,
        in_specs=[pl.BlockSpec(memory_space=pltpu.VMEM)] * 6,
        out_specs=pl.BlockSpec(memory_space=pltpu.VMEM),
        out_shape=jax.ShapeDtypeStruct((ROWS, LAT), jnp.bfloat16),
        scratch_shapes=[
            pltpu.VMEM((PAGE // 4, ROWS, wide), jnp.float32),
            pltpu.VMEM((ROWS, 128), jnp.float32),
            pltpu.VMEM((ROWS, wide), jnp.float32),
            pltpu.VMEM((ROWS, wide), jnp.float32),
            pltpu.VMEM((ROWS, LAT), jnp.float32),
            pltpu.VMEM((ROWS, KPAD), jnp.float32),
            pltpu.VMEM((ROWS, 2 * wide), jnp.bfloat16),
        ],
        compiler_params=params(),
        cost_estimate=pl.CostEstimate(
            flops=20_000_000_000, bytes_accessed=10_000_000, transcendentals=4_000_000
        ),
    )(kv_cache, *operands)
    return out.reshape(STEPS, REQ, H * LAT)


def leaving_pages(kv_cache, moved_slot, moved_target):
    groups = lax.axis_size("dp")
    width = kv_cache.shape[1]
    named = jnp.arange(groups, dtype=jnp.int32)[:, None, None] == moved_target[:, 0][None, :, None]
    from_slot = moved_slot[None, :, None] == jnp.arange(SLOTS, dtype=jnp.int32)[None, None, :]
    placing = jnp.any(named & from_slot, axis=1).astype(jnp.bfloat16)
    leaving = jnp.dot(placing, kv_cache, preferred_element_type=jnp.float32).astype(jnp.bfloat16)
    return leaving.reshape(groups, width // 128, 128)


Hooks = collections.namedtuple("Hooks", "operands leaving")


def body(kv_cache, slot_fill, slot_request, moved_slot, moved_target, queries, new_kv,
         expert_input, expert_ids, gate_weights, w_gate, w_up, down_weight):
    hooks = Hooks(attention_operands, functools.partial(leaving_pages, kv_cache))
    expert_out, guest_pages, ready = experts(
        expert_input, expert_ids, gate_weights, w_gate, w_up, down_weight, hooks,
        (moved_slot, moved_target), (slot_fill, slot_request, queries, new_kv),
    )
    attention_out = attention(kv_cache, ready)
    return guest_pages, attention_out, expert_out


def solution(mesh):
    rows = P(("dp", "ep"), None)
    flat = P(("dp", "ep"))
    second = P(None, ("dp", "ep"), None)
    return jax.shard_map(
        body,
        mesh=mesh,
        in_specs=(rows, flat, flat, flat, rows, second, second, second, second, second,
                  P("dp", None, "ep"), P("dp", None, "ep"), P("dp", "ep", None)),
        out_specs=(rows, second, second),
        check_vma=False,
    )
```

profile of v0, /device:TPU:1, one launch (start us, length us, event | category | flops | bytes accessed | tf_op | source)
XLA Modules:
  0.0 167.0 jit_solution(11502140021619852673)
XLA Ops:
  4.2 3.4 %constant_dynamic-slice_fusion.2 = (bf16[2,256,896]{2,1,0:T(8,128)(2,1)}, bf16[2,256,896]{2,1,0:T(8,128)(2,1)}, bf16[2,256,896]{2,1,0:T(8,128)(2,1)}) fusion(bf16[2,256,3584]{2,1,0:T(8,128)(2,1)} %param.25, s32[]{:T(128)S(6)} %select_n.64, s32[]{:T(128)S(6)} %select_n.62, s32[]{:T(128)S(6)} %select_n.61), kind=kLoop, calls=%fused_computation.28 | loop fusion | bytes 5505036 | tf_op jit(solution)/shard_map/dynamic_slice | solution.py:222
  9.0 2.6 %collective-permute-start.2 = (bf16[16,3712]{1,0:T(8,128)(2,1)S(1)}, bf16[16,3712]{1,0:T(8,128)(2,1)S(1)}, u32[]{:S(2)}, u32[]{:S(2)}) collective-permute-start(bf16[16,3712]{1,0:T(8,128)(2,1)S(1)} %maximum_select_fusion), channel_id=1, source_target_pairs={{0,2},{1,3},{2,0},{3,1},{4,6},{5,7},{6,4},{7,5},{8,10},{9,11},{10,... | collective-permute-start | bytes 356360 | tf_op jit(solution)/shard_map/ppermute | solution.py:196
  12.7 2.0 %constant_dynamic-slice_fusion = (bf16[1,256,896]{2,1,0:T(8,128)(2,1)S(1)}, bf16[1,256,896]{2,1,0:T(8,128)(2,1)}) fusion(bf16[2,256,3584]{2,1,0:T(8,128)(2,1)} %param.25, s32[]{:T(128)S(6)} %add.56, s32[]{:T(128)S(6)} %select_n.63), kind=kLoop, calls=%fused_computation.26 | loop fusion | bytes 1835016 | tf_op jit(solution)/shard_map/slice | solution.py:245
  15.3 2.2 %collective-permute-done.2 = bf16[16,3712]{1,0:T(8,128)(2,1)S(1)} collective-permute-done((bf16[16,3712]{1,0:T(8,128)(2,1)S(1)}, bf16[16,3712]{1,0:T(8,128)(2,1)S(1)}, u32[]{:S(2)}, u32[]{:S(2)}) %collective-permute-start.2) | collective-permute-done | bytes 118816 | tf_op jit(solution)/shard_map/ppermute | solution.py:196
  19.3 3.3 %collective-permute-start.5 = (bf16[64,3712]{1,0:T(8,128)(2,1)S(1)}, bf16[64,3712]{1,0:T(8,128)(2,1)}, u32[]{:S(2)}, u32[]{:S(2)}) collective-permute-start(bf16[64,3712]{1,0:T(8,128)(2,1)S(1)} %pad_maximum_fusion.1), channel_id=1, source_target_pairs={{0,64},{4,20},{8,72},{12,28},{16,80},{20,4},{24,88},{28,12},{32,96... | collective-permute-start | bytes 1425416 | tf_op jit(solution)/shard_map/ppermute | solution.py:203
  25.4 2.1 %collective-permute-start.7 = (bf16[1,256,896]{2,1,0:T(8,128)(2,1)}, bf16[1,256,896]{2,1,0:T(8,128)(2,1)}, u32[]{:S(2)}, u32[]{:S(2)}) collective-permute-start(bf16[1,256,896]{2,1,0:T(8,128)(2,1)} %get-tuple-element.52), channel_id=1, source_target_pairs={{0,2},{1,3},{2,0},{3,1},{4,6},{5,7},{6,4},{7,5},{8,10},{9,11},{10,... | collective-permute-start | bytes 1376264 | tf_op jit(solution)/shard_map/ppermute | solution.py:196
  31.5 2.3 %fusion.7 = (bf16[1024,640]{1,0:T(8,128)(2,1)}, bf16[1024,640]{1,0:T(8,128)(2,1)}) fusion(bf16[1024,576]{1,0:T(8,128)(2,1)S(1)} %reshape.127), kind=kLoop, calls=%fused_computation.32 | loop fusion | bytes 3801088 | tf_op jit(solution)/shard_map/jit(_pad)/pad | solution.py:364
  35.6 2.9 %collective-permute-done.7.refs_11_ = bf16[1,256,896]{2,1,0:T(8,128)(2,1)} collective-permute-done((bf16[1,256,896]{2,1,0:T(8,128)(2,1)}, bf16[1,256,896]{2,1,0:T(8,128)(2,1)}, u32[]{:S(2)}, u32[]{:S(2)}) %collective-permute-start.7) | collective-permute-done | bytes 458784 | tf_op jit(solution)/shard_map/ppermute | solution.py:196
  43.5 2.1 %collective-permute-start.12 = (bf16[2,256,896]{2,1,0:T(8,128)(2,1)}, bf16[2,256,896]{2,1,0:T(8,128)(2,1)}, u32[]{:S(2)}, u32[]{:S(2)}) collective-permute-start(bf16[2,256,896]{2,1,0:T(8,128)(2,1)} %get-tuple-element.57), channel_id=1, source_target_pairs={{0,3},{1,0},{2,1},{3,2},{4,7},{5,4},{6,5},{7,6},{8,11},{9,8},{10,9... | collective-permute-start | bytes 2752520 | tf_op jit(solution)/shard_map/ppermute | solution.py:196
  45.8 3.1 %fusion = bf16[4,8,288,128]{3,1,2,0:T(8,128)(2,1)S(1)} fusion(pred[32,64]{1,0:T(8,128)(4,1)S(1)} %and_reduce_fusion, bf16[64,36864]{1,0:T(8,128)(2,1)} %kv_ref.1), kind=kOutput, calls=%fused_computation.3 | convolution fusion | flops 152174592 | bytes 7079936 | tf_op jit(solution)/shard_map/dot_general | solution.py:401
  51.9 6.9 %shard_map.148.refs_6_ = bf16[2,128,256]{2,1,0:T(8,128)(2,1)} custom-call(s32[5]{0:T(128)} %stack.23.place_ref, bf16[256,3712]{1,0:T(8,128)(2,1)} %copy-done, bf16[256,3712]{1,0:T(8,128)(2,1)} %copy-done.3, bf16[2,3584,256]{2,1,0:T(8,128)(2,1)} %refs_4_.3, bf16[2,3584,256]{2,1,0:T(8,128)(2,1)} %refs_5_.3), custom_call_target="tpu_custom_call" | custom-call | flops 2000000000 | bytes 11500000 | tf_op jit(solution)/shard_map/pallas_call | solution.py:83
  58.9 6.9 %collective-permute-done.11.refs_9_ = bf16[2,256,896]{2,1,0:T(8,128)(2,1)} collective-permute-done((bf16[2,256,896]{2,1,0:T(8,128)(2,1)}, bf16[2,256,896]{2,1,0:T(8,128)(2,1)}, u32[]{:S(2)}, u32[]{:S(2)}) %collective-permute-start.11) | collective-permute-done | bytes 917536 | tf_op jit(solution)/shard_map/ppermute | solution.py:196
  69.5 2.7 %collective-permute-start.14 = (bf16[128,3712]{1,0:T(8,128)(2,1)}, bf16[128,3712]{1,0:T(8,128)(2,1)}, u32[]{:S(2)}, u32[]{:S(2)}) collective-permute-start(bf16[128,3712]{1,0:T(8,128)(2,1)} %slice.23), channel_id=1, source_target_pairs={{0,24},{4,100},{8,0},{12,108},{16,8},{20,116},{24,16},{28,124},{32... | collective-permute-start | bytes 2850824 | tf_op jit(solution)/shard_map/ppermute | solution.py:203
  76.5 10.0 %shard_map.149.refs_0_ = bf16[2,384,256]{2,1,0:T(8,128)(2,1)} custom-call(s32[5]{0:T(128)} %stack.23.place_ref, bf16[256,3712]{1,0:T(8,128)(2,1)} %copy-done.1, bf16[256,3712]{1,0:T(8,128)(2,1)} %copy-done.4, bf16[256,3712]{1,0:T(8,128)(2,1)} %copy-done.2, bf16[256,3712]{1,0:T(8,128)(2,1)} %copy-done.5, bf16[2,3584,256]{2,1,0:T(8,128)(2,1)} %refs_4_.3, ...), custom_call_target="tpu_custom_call" | custom-call | flops 4000000000 | bytes 15500000 | tf_op jit(solution)/shard_map/pallas_call | solution.py:83
  86.5 5.5 %all-to-all-start = ((bf16[32,288,128]{2,1,0:T(8,128)(2,1)}), bf16[32,288,128]{2,1,0:T(8,128)(2,1)S(1)}, u32[]{:S(2)}, u32[]{:S(2)}) async-start(bf16[32,288,128]{2,1,0:T(8,128)(2,1)} %bitcast.14), calls=%async_computation | async-start | bytes 4718592 | tf_op jit(solution)/shard_map/all_to_all | solution.py:271
  97.7 6.9 %shard_map.151.refs_4_ = bf16[2,128,256]{2,1,0:T(8,128)(2,1)} custom-call(s32[5]{0:T(128)} %stack.23.place_ref, bf16[128,3712]{1,0:T(8,128)(2,1)} %collective-permute-done.13.refs_0_, bf16[128,3712]{1,0:T(8,128)(2,1)} %collective-permute-done.14.refs_1_, bf16[128,3712]{1,0:T(8,128)(2,1)} %copy-done.7, bf16[128,3712]{1,0:T(8,128)(2,1)} %copy-done.8, ...), custom_call_target="tpu_custom_call" | custom-call | flops 2000000000 | bytes 11500000 | tf_op jit(solution)/shard_map/pallas_call | solution.py:83
  109.2 3.1 %collective-permute-done.20.refs_3_ = bf16[2,384,256]{2,1,0:T(8,128)(2,1)} collective-permute-done((bf16[2,384,256]{2,1,0:T(8,128)(2,1)S(1)}, bf16[2,384,256]{2,1,0:T(8,128)(2,1)}, u32[]{:S(2)}, u32[]{:S(2)}) %collective-permute-start.20) | collective-permute-done | bytes 393248 | tf_op jit(solution)/shard_map/ppermute | solution.py:196
  112.3 5.0 %collective-permute-done.23.refs_5_ = bf16[2,128,256]{2,1,0:T(8,128)(2,1)S(1)} collective-permute-done((bf16[2,128,256]{2,1,0:T(8,128)(2,1)}, bf16[2,128,256]{2,1,0:T(8,128)(2,1)S(1)}, u32[]{:S(2)}, u32[]{:S(2)}) %collective-permute-start.23) | collective-permute-done | bytes 131104 | tf_op jit(solution)/shard_map/ppermute | solution.py:196
  118.0 7.2 %shard_map.152 = bf16[128,8,896]{2,1,0:T(8,128)(2,1)} custom-call(s32[5]{0:T(128)} %stack.23.place_ref, bf16[2,384,256]{2,1,0:T(8,128)(2,1)} %shard_map.149.refs_0_, bf16[2,384,256]{2,1,0:T(8,128)(2,1)} %copy-done.14, bf16[2,384,256]{2,1,0:T(8,128)(2,1)} %collective-permute-done.19.refs_2_, bf16[2,384,256]{2,1,0:T(8,128)(2,1)} %collective-permute-done.20.refs_3_, ...), custom_call_target="tpu_custom_call" | custom-call | flops 3000000000 | bytes 8000000 | tf_op jit(solution)/shard_map/pallas_call | solution.py:138
  125.2 10.9 %all-to-all-start.1 = ((bf16[128,8,896]{2,1,0:T(8,128)(2,1)}), bf16[128,8,896]{2,1,0:T(8,128)(2,1)}, u32[]{:S(2)}, u32[]{:S(2)}) async-start(bf16[128,8,896]{2,1,0:T(8,128)(2,1)} %shard_map.152), calls=%async_computation.1 | async-start | bytes 3670016 | tf_op jit(solution)/shard_map/all_to_all | solution.py:277
  136.1 22.0 %shard_map.150 = bf16[1024,512]{1,0:T(8,128)(2,1)} custom-call(bf16[64,36864]{1,0:T(8,128)(2,1)} %kv_ref.1, bf16[1024,640]{1,0:T(8,128)(2,1)} %get-tuple-element.68.qe_ref, bf16[1024,640]{1,0:T(8,128)(2,1)} %get-tuple-element.69.qo_ref, bf16[128,640]{1,0:T(8,128)(2,1)} %pad.19.fresh_ref, s32[1,256]{1,0:T(1,128)} %reshape_tile.6.fill_ref, ...), custom_call_target="tpu_custom_call" | custom-call | flops 20000000000 | bytes 10000000 | tf_op jit(solution)/shard_map/pallas_call | solution.py:373
  158.1 2.6 %reshape.131 = bf16[2,4,65536]{2,1,0:T(4,128)(2,1)} reshape(bf16[1024,512]{1,0:T(8,128)(2,1)} %shard_map.150) | data formatting | bytes 2097152 | tf_op jit(solution)/shard_map/reshape | solution.py:392
  160.8 2.3 %copy.29 = bf16[4,8,288,128]{3,1,2,0:T(8,128)(2,1)} copy(bf16[4,8,288,128]{3,2,1,0:T(8,128)(2,1)S(1)} %bitcast.31) | data formatting | bytes 4718592
  164.0 3.0 %shard_map.153 = bf16[2,8,3584]{2,1,0:T(8,128)(2,1)} custom-call(f32[16,256]{1,0:T(8,128)} %copy.25.mix_ref, bf16[32,4,8,896]{3,2,1,0:T(8,128)(2,1)} %bitcast.11.ret_ref), custom_call_target="tpu_custom_call" | custom-call | tf_op jit(solution)/shard_map/pallas_call | solution.py:172
  (111 shorter events, 45.0 us)
Async XLA Ops:
  7.6 7.8 %collective-permute-start.1 = (bf16[16,3712]{1,0:T(8,128)(2,1)S(1)}, bf16[16,3712]{1,0:T(8,128)(2,1)S(1)}, u32[]{:S(2)}, u32[]{:S(2)}) collective-permute-start(bf16[16,3712]{1,0:T(8,128)(2,1)S(1)} %maximum_select_fusion), channel_id=1, source_target_pairs={{0,1},{1,2},{2,3},{3,0},{4,5},{5,6},{6,7},{7,4},{8,9},{9,10},{10,1... | collective-permute-start | bytes 356360 | tf_op jit(solution)/shard_map/ppermute | solution.py:196
  9.0 8.5 %collective-permute-start.2 = (bf16[16,3712]{1,0:T(8,128)(2,1)S(1)}, bf16[16,3712]{1,0:T(8,128)(2,1)S(1)}, u32[]{:S(2)}, u32[]{:S(2)}) collective-permute-start(bf16[16,3712]{1,0:T(8,128)(2,1)S(1)} %maximum_select_fusion), channel_id=1, source_target_pairs={{0,2},{1,3},{2,0},{3,1},{4,6},{5,7},{6,4},{7,5},{8,10},{9,11},{10,... | collective-permute-start | bytes 356360 | tf_op jit(solution)/shard_map/ppermute | solution.py:196
  17.6 16.2 %collective-permute-start.4 = (bf16[64,3712]{1,0:T(8,128)(2,1)S(1)}, bf16[64,3712]{1,0:T(8,128)(2,1)}, u32[]{:S(2)}, u32[]{:S(2)}) collective-permute-start(bf16[64,3712]{1,0:T(8,128)(2,1)S(1)} %pad_maximum_fusion.1), channel_id=1, source_target_pairs={{0,32},{4,12},{8,40},{12,20},{16,48},{20,28},{24,56},{28,4},{32,64... | collective-permute-start | bytes 1425416 | tf_op jit(solution)/shard_map/ppermute | solution.py:203
  19.3 14.8 %collective-permute-start.5 = (bf16[64,3712]{1,0:T(8,128)(2,1)S(1)}, bf16[64,3712]{1,0:T(8,128)(2,1)}, u32[]{:S(2)}, u32[]{:S(2)}) collective-permute-start(bf16[64,3712]{1,0:T(8,128)(2,1)S(1)} %pad_maximum_fusion.1), channel_id=1, source_target_pairs={{0,64},{4,20},{8,72},{12,28},{16,80},{20,4},{24,88},{28,12},{32,96... | collective-permute-start | bytes 1425416 | tf_op jit(solution)/shard_map/ppermute | solution.py:203
  22.6 11.5 %collective-permute-start.6 = (bf16[64,3712]{1,0:T(8,128)(2,1)S(1)}, bf16[64,3712]{1,0:T(8,128)(2,1)}, u32[]{:S(2)}, u32[]{:S(2)}) collective-permute-start(bf16[64,3712]{1,0:T(8,128)(2,1)S(1)} %pad_maximum_fusion.1), channel_id=1, source_target_pairs={{0,96},{4,28},{8,104},{12,4},{16,112},{20,12},{24,120},{28,20},{32... | collective-permute-start | bytes 1425416 | tf_op jit(solution)/shard_map/ppermute | solution.py:203
  25.4 13.1 %collective-permute-start.7 = (bf16[1,256,896]{2,1,0:T(8,128)(2,1)}, bf16[1,256,896]{2,1,0:T(8,128)(2,1)}, u32[]{:S(2)}, u32[]{:S(2)}) collective-permute-start(bf16[1,256,896]{2,1,0:T(8,128)(2,1)} %get-tuple-element.52), channel_id=1, source_target_pairs={{0,2},{1,3},{2,0},{3,1},{4,6},{5,7},{6,4},{7,5},{8,10},{9,11},{10,... | collective-permute-start | bytes 1376264 | tf_op jit(solution)/shard_map/ppermute | solution.py:196
  38.5 12.1 %collective-permute-start.10 = (bf16[256,3712]{1,0:T(8,128)(2,1)S(1)}, bf16[256,3712]{1,0:T(8,128)(2,1)S(1)}, u32[]{:S(2)}, u32[]{:S(2)}) collective-permute-start(bf16[256,3712]{1,0:T(8,128)(2,1)S(1)} %pad_maximum_fusion.refs_0_), channel_id=1, source_target_pairs={{0,4},{4,0},{8,12},{12,8},{16,20},{20,16},{24,28},{28,24},{32,36},... | collective-permute-start | bytes 5701640 | tf_op jit(solution)/shard_map/ppermute | solution.py:203
  40.2 25.6 %collective-permute-start.8 = (bf16[256,3712]{1,0:T(8,128)(2,1)S(1)}, bf16[256,3712]{1,0:T(8,128)(2,1)S(1)}, u32[]{:S(2)}, u32[]{:S(2)}) collective-permute-start(bf16[256,3712]{1,0:T(8,128)(2,1)S(1)} %pad_maximum_fusion.refs_0_), channel_id=1, source_target_pairs={{0,8},{4,36},{8,16},{12,44},{16,24},{20,52},{24,0},{28,60},{32,40}... | collective-permute-start | bytes 5701640 | tf_op jit(solution)/shard_map/ppermute | solution.py:203
  41.5 24.4 %collective-permute-start.9 = (bf16[256,3712]{1,0:T(8,128)(2,1)S(1)}, bf16[256,3712]{1,0:T(8,128)(2,1)S(1)}, u32[]{:S(2)}, u32[]{:S(2)}) collective-permute-start(bf16[256,3712]{1,0:T(8,128)(2,1)S(1)} %pad_maximum_fusion.refs_0_), channel_id=1, source_target_pairs={{0,24},{4,100},{8,0},{12,108},{16,8},{20,116},{24,16},{28,124},{32... | collective-permute-start | bytes 5701640 | tf_op jit(solution)/shard_map/ppermute | solution.py:203
  42.9 22.9 %collective-permute-start.11 = (bf16[2,256,896]{2,1,0:T(8,128)(2,1)}, bf16[2,256,896]{2,1,0:T(8,128)(2,1)}, u32[]{:S(2)}, u32[]{:S(2)}) collective-permute-start(bf16[2,256,896]{2,1,0:T(8,128)(2,1)} %get-tuple-element.56), channel_id=1, source_target_pairs={{0,1},{1,2},{2,3},{3,0},{4,5},{5,6},{6,7},{7,4},{8,9},{9,10},{10,1... | collective-permute-start | bytes 2752520 | tf_op jit(solution)/shard_map/ppermute | solution.py:196
  43.5 22.3 %collective-permute-start.12 = (bf16[2,256,896]{2,1,0:T(8,128)(2,1)}, bf16[2,256,896]{2,1,0:T(8,128)(2,1)}, u32[]{:S(2)}, u32[]{:S(2)}) collective-permute-start(bf16[2,256,896]{2,1,0:T(8,128)(2,1)} %get-tuple-element.57), channel_id=1, source_target_pairs={{0,3},{1,0},{2,1},{3,2},{4,7},{5,4},{6,5},{7,6},{8,11},{9,8},{10,9... | collective-permute-start | bytes 2752520 | tf_op jit(solution)/shard_map/ppermute | solution.py:196
  65.8 8.2 %collective-permute-start.15 = (bf16[256,3712]{1,0:T(8,128)(2,1)S(1)}, bf16[256,3712]{1,0:T(8,128)(2,1)S(1)}, u32[]{:S(2)}, u32[]{:S(2)}) collective-permute-start(bf16[256,3712]{1,0:T(8,128)(2,1)S(1)} %collective-permute-done.8.refs_0_), channel_id=1, source_target_pairs={{0,4},{4,0},{8,12},{12,8},{16,20},{20,16},{24,28},{28,24},{32,36},... | collective-permute-start | bytes 5701640 | tf_op jit(solution)/shard_map/ppermute | solution.py:203
  67.3 6.7 %collective-permute-start.16 = (bf16[256,3712]{1,0:T(8,128)(2,1)S(1)}, bf16[256,3712]{1,0:T(8,128)(2,1)S(1)}, u32[]{:S(2)}, u32[]{:S(2)}) collective-permute-start(bf16[256,3712]{1,0:T(8,128)(2,1)S(1)} %collective-permute-done.9.refs_2_), channel_id=1, source_target_pairs={{0,4},{4,0},{8,12},{12,8},{16,20},{20,16},{24,28},{28,24},{32,36},... | collective-permute-start | bytes 5701640 | tf_op jit(solution)/shard_map/ppermute | solution.py:203
  69.5 17.0 %collective-permute-start.13 = (bf16[128,3712]{1,0:T(8,128)(2,1)}, bf16[128,3712]{1,0:T(8,128)(2,1)}, u32[]{:S(2)}, u32[]{:S(2)}) collective-permute-start(bf16[128,3712]{1,0:T(8,128)(2,1)} %slice.22), channel_id=1, source_target_pairs={{0,8},{4,36},{8,16},{12,44},{16,24},{20,52},{24,0},{28,60},{32,40}... | collective-permute-start | bytes 2850824 | tf_op jit(solution)/shard_map/ppermute | solution.py:203
  69.5 17.0 %collective-permute-start.14 = (bf16[128,3712]{1,0:T(8,128)(2,1)}, bf16[128,3712]{1,0:T(8,128)(2,1)}, u32[]{:S(2)}, u32[]{:S(2)}) collective-permute-start(bf16[128,3712]{1,0:T(8,128)(2,1)} %slice.23), channel_id=1, source_target_pairs={{0,24},{4,100},{8,0},{12,108},{16,8},{20,116},{24,16},{28,124},{32... | collective-permute-start | bytes 2850824 | tf_op jit(solution)/shard_map/ppermute | solution.py:203
  72.2 14.3 %collective-permute-start.17 = (bf16[1,256,896]{2,1,0:T(8,128)(2,1)S(1)}, bf16[1,256,896]{2,1,0:T(8,128)(2,1)}, u32[]{:S(2)}, u32[]{:S(2)}) collective-permute-start(bf16[1,256,896]{2,1,0:T(8,128)(2,1)S(1)} %get-tuple-element.65), channel_id=1, source_target_pairs={{0,2},{1,3},{2,0},{3,1},{4,6},{5,7},{6,4},{7,5},{8,10},{9,11},{10,... | collective-permute-start | bytes 1376264 | tf_op jit(solution)/shard_map/ppermute | solution.py:196
  86.5 38.7 %all-to-all-start = ((bf16[32,288,128]{2,1,0:T(8,128)(2,1)}), bf16[32,288,128]{2,1,0:T(8,128)(2,1)S(1)}, u32[]{:S(2)}, u32[]{:S(2)}) async-start(bf16[32,288,128]{2,1,0:T(8,128)(2,1)} %bitcast.14), calls=%async_computation | async-start | bytes 4718592 | tf_op jit(solution)/shard_map/all_to_all | solution.py:271
  92.6 14.7 %collective-permute-start.18 = (bf16[2,384,256]{2,1,0:T(8,128)(2,1)S(1)}, bf16[2,384,256]{2,1,0:T(8,128)(2,1)S(1)}, u32[]{:S(2)}, u32[]{:S(2)}) collective-permute-start(bf16[2,384,256]{2,1,0:T(8,128)(2,1)S(1)} %copy-done.9), channel_id=1, source_target_pairs={{0,1},{1,2},{2,3},{3,0},{4,5},{5,6},{6,7},{7,4},{8,9},{9,10},{10,1... | collective-permute-start | bytes 1179656 | tf_op jit(solution)/shard_map/ppermute | solution.py:196
  94.1 15.2 %collective-permute-start.19 = (bf16[2,384,256]{2,1,0:T(8,128)(2,1)S(1)}, bf16[2,384,256]{2,1,0:T(8,128)(2,1)}, u32[]{:S(2)}, u32[]{:S(2)}) collective-permute-start(bf16[2,384,256]{2,1,0:T(8,128)(2,1)S(1)} %copy-done.9), channel_id=1, source_target_pairs={{0,3},{1,0},{2,1},{3,2},{4,7},{5,4},{6,5},{7,6},{8,11},{9,8},{10,9... | collective-permute-start | bytes 1179656 | tf_op jit(solution)/shard_map/ppermute | solution.py:196
  95.3 17.0 %collective-permute-start.20 = (bf16[2,384,256]{2,1,0:T(8,128)(2,1)S(1)}, bf16[2,384,256]{2,1,0:T(8,128)(2,1)}, u32[]{:S(2)}, u32[]{:S(2)}) collective-permute-start(bf16[2,384,256]{2,1,0:T(8,128)(2,1)S(1)} %copy-done.9), channel_id=1, source_target_pairs={{0,2},{1,3},{2,0},{3,1},{4,6},{5,7},{6,4},{7,5},{8,10},{9,11},{10,... | collective-permute-start | bytes 1179656 | tf_op jit(solution)/shard_map/ppermute | solution.py:196
  104.7 12.7 %collective-permute-start.23 = (bf16[2,128,256]{2,1,0:T(8,128)(2,1)}, bf16[2,128,256]{2,1,0:T(8,128)(2,1)S(1)}, u32[]{:S(2)}, u32[]{:S(2)}) collective-permute-start(bf16[2,128,256]{2,1,0:T(8,128)(2,1)} %shard_map.151.refs_4_), channel_id=1, source_target_pairs={{0,1},{1,2},{2,3},{3,0},{4,5},{5,6},{6,7},{7,4},{8,9},{9,10},{10,1... | collective-permute-start | bytes 393224 | tf_op jit(solution)/shard_map/ppermute | solution.py:196
  105.5 11.8 %collective-permute-start.24 = (bf16[2,128,256]{2,1,0:T(8,128)(2,1)}, bf16[2,128,256]{2,1,0:T(8,128)(2,1)}, u32[]{:S(2)}, u32[]{:S(2)}) collective-permute-start(bf16[2,128,256]{2,1,0:T(8,128)(2,1)} %shard_map.151.refs_4_), channel_id=1, source_target_pairs={{0,3},{1,0},{2,1},{3,2},{4,7},{5,4},{6,5},{7,6},{8,11},{9,8},{10,9... | collective-permute-start | bytes 393224 | tf_op jit(solution)/shard_map/ppermute | solution.py:196
  107.3 10.0 %collective-permute-start.25 = (bf16[2,128,256]{2,1,0:T(8,128)(2,1)}, bf16[2,128,256]{2,1,0:T(8,128)(2,1)}, u32[]{:S(2)}, u32[]{:S(2)}) collective-permute-start(bf16[2,128,256]{2,1,0:T(8,128)(2,1)} %shard_map.151.refs_4_), channel_id=1, source_target_pairs={{0,2},{1,3},{2,0},{3,1},{4,6},{5,7},{6,4},{7,5},{8,10},{9,11},{10,... | collective-permute-start | bytes 393224 | tf_op jit(solution)/shard_map/ppermute | solution.py:196
  125.2 38.8 %all-to-all-start.1 = ((bf16[128,8,896]{2,1,0:T(8,128)(2,1)}), bf16[128,8,896]{2,1,0:T(8,128)(2,1)}, u32[]{:S(2)}, u32[]{:S(2)}) async-start(bf16[128,8,896]{2,1,0:T(8,128)(2,1)} %shard_map.152), calls=%async_computation.1 | async-start | bytes 3670016 | tf_op jit(solution)/shard_map/all_to_all | solution.py:277
  (20 other events, 142.5 us)
where the time goes:
time: 168 us; the launch traced here: 167 us
  Pallas kernels  56 us (33%)
  starting transfers between devices  51.7 us (31%)
  local copies, waits for them, and re-layouts  29.5 us (18%)
  waiting for transfers between devices  21.8 us (13%)
  other arithmetic  3.91 us (2%)
  matrix products  3.09 us (2%)
    pallas_call x3, Pallas kernels, inner_of(): pl.pallas_call(functools.partial(inner_kernel, kinds, len(pieces) // n),...  23.8 us
    pallas_call x1, Pallas kernels, attention(): pl.pallas_call(attention_kernel, in_specs=[pl.BlockSpec(memory_space=pltp...  22 us
    ppermute x13, waiting for transfers between devices, over_ep(): lax.ppermute(array, 'ep', [(i, (i + k) % ranks) for i in range(ranks)])  20.2 us
    ppermute x13, starting transfers between devices, over_ep(): lax.ppermute(array, 'ep', [(i, (i + k) % ranks) for i in range(ranks)])  18.8 us
    ppermute x13, starting transfers between devices, over_dp(): return lax.ppermute(array, 'dp', pairs)  16.5 us
    all_to_all x1, starting transfers between devices, experts(): lax.all_to_all(produced, ('dp', 'ep'), split_axis=0, concat_axis=0, tiled...  10.9 us
    unnamed x34, local copies, waits for them, and re-layouts  10 us
    pallas_call x1, Pallas kernels, down_of(): pl.pallas_call(down_kernel, in_specs=[pl.BlockSpec(memory_space=pltpu.SME...  7.21 us
  transfers between devices with their start and end apart: 28, of which 8 were waited for; matrix products, arithmetic and copies ran while one was open for 17% of the time, Pallas kernels for 32%

commit v1 on v0

--- a/solution.py
+++ b/solution.py
@@ -158,11 +158,11 @@
     mid = rest.astype(jnp.bfloat16)
     low = (rest - mid.astype(jnp.float32)).astype(jnp.bfloat16)
     tokens = mix.shape[0]
+    three = jnp.concatenate([high, mid, low], axis=0)
     for q in range(4):
         rows = ret_ref[:, q].astype(jnp.float32).reshape(-1, DQ).astype(jnp.bfloat16)
-        total = jnp.dot(high, rows, preferred_element_type=jnp.float32)
-        total = total + jnp.dot(mid, rows, preferred_element_type=jnp.float32)
-        total = total + jnp.dot(low, rows, preferred_element_type=jnp.float32)
+        total = jnp.dot(three, rows, preferred_element_type=jnp.float32)
+        total = total[:tokens] + total[tokens : 2 * tokens] + total[2 * tokens :]
         total = total.astype(jnp.bfloat16)
         for s in range(STEPS):
             o_ref[s, :, q * DQ : (q + 1) * DQ] = total[s * TOK : (s + 1) * TOK]

time: 168 us -> 167 us (level)
  no operation moved by 1% of the time
where the time goes in v1:
time: 167 us
  Pallas kernels  55.6 us (33%)
  starting transfers between devices  51.7 us (31%)
  local copies, waits for them, and re-layouts  29.5 us (18%)
  waiting for transfers between devices  21.8 us (13%)
  other arithmetic  3.91 us (2%)
  matrix products  3.09 us (2%)
    pallas_call x3, Pallas kernels, inner_of(): pl.pallas_call(functools.partial(inner_kernel, kinds, len(pieces) // n),...  23.8 us
    pallas_call x1, Pallas kernels, attention(): pl.pallas_call(attention_kernel, in_specs=[pl.BlockSpec(memory_space=pltp...  22 us
    ppermute x13, waiting for transfers between devices, over_ep(): lax.ppermute(array, 'ep', [(i, (i + k) % ranks) for i in range(ranks)])  20.2 us
    ppermute x13, starting transfers between devices, over_ep(): lax.ppermute(array, 'ep', [(i, (i + k) % ranks) for i in range(ranks)])  18.8 us
    ppermute x13, starting transfers between devices, over_dp(): return lax.ppermute(array, 'dp', pairs)  16.5 us
    all_to_all x1, starting transfers between devices, experts(): lax.all_to_all(produced, ('dp', 'ep'), split_axis=0, concat_axis=0, tiled...  10.9 us
    unnamed x34, local copies, waits for them, and re-layouts  10 us
    pallas_call x1, Pallas kernels, down_of(): pl.pallas_call(down_kernel, in_specs=[pl.BlockSpec(memory_space=pltpu.SME...  7.21 us
  transfers between devices with their start and end apart: 28, of which 8 were waited for; matrix products, arithmetic and copies ran while one was open for 17% of the time, Pallas kernels for 32%

profile of v1, /device:TPU:1, one launch (start us, length us, event | category | flops | bytes accessed | tf_op | source)
XLA Modules:
  0.0 166.6 jit_solution(10973393919507537128)
XLA Ops:
  4.2 3.4 %constant_dynamic-slice_fusion.2 = (bf16[2,256,896]{2,1,0:T(8,128)(2,1)}, bf16[2,256,896]{2,1,0:T(8,128)(2,1)}, bf16[2,256,896]{2,1,0:T(8,128)(2,1)}) fusion(bf16[2,256,3584]{2,1,0:T(8,128)(2,1)} %param.25, s32[]{:T(128)S(6)} %select_n.64, s32[]{:T(128)S(6)} %select_n.62, s32[]{:T(128)S(6)} %select_n.61), kind=kLoop, calls=%fused_computation.28 | loop fusion | bytes 5505036 | tf_op jit(solution)/shard_map/dynamic_slice | solution.py:222
  9.0 2.6 %collective-permute-start.2 = (bf16[16,3712]{1,0:T(8,128)(2,1)S(1)}, bf16[16,3712]{1,0:T(8,128)(2,1)S(1)}, u32[]{:S(2)}, u32[]{:S(2)}) collective-permute-start(bf16[16,3712]{1,0:T(8,128)(2,1)S(1)} %maximum_select_fusion), channel_id=1, source_target_pairs={{0,2},{1,3},{2,0},{3,1},{4,6},{5,7},{6,4},{7,5},{8,10},{9,11},{10,... | collective-permute-start | bytes 356360 | tf_op jit(solution)/shard_map/ppermute | solution.py:196
  12.7 2.0 %constant_dynamic-slice_fusion = (bf16[1,256,896]{2,1,0:T(8,128)(2,1)S(1)}, bf16[1,256,896]{2,1,0:T(8,128)(2,1)}) fusion(bf16[2,256,3584]{2,1,0:T(8,128)(2,1)} %param.25, s32[]{:T(128)S(6)} %add.56, s32[]{:T(128)S(6)} %select_n.63), kind=kLoop, calls=%fused_computation.26 | loop fusion | bytes 1835016 | tf_op jit(solution)/shard_map/slice | solution.py:245
  15.3 2.2 %collective-permute-done.2 = bf16[16,3712]{1,0:T(8,128)(2,1)S(1)} collective-permute-done((bf16[16,3712]{1,0:T(8,128)(2,1)S(1)}, bf16[16,3712]{1,0:T(8,128)(2,1)S(1)}, u32[]{:S(2)}, u32[]{:S(2)}) %collective-permute-start.2) | collective-permute-done | bytes 118816 | tf_op jit(solution)/shard_map/ppermute | solution.py:196
  19.3 3.3 %collective-permute-start.5 = (bf16[64,3712]{1,0:T(8,128)(2,1)S(1)}, bf16[64,3712]{1,0:T(8,128)(2,1)}, u32[]{:S(2)}, u32[]{:S(2)}) collective-permute-start(bf16[64,3712]{1,0:T(8,128)(2,1)S(1)} %pad_maximum_fusion.1), channel_id=1, source_target_pairs={{0,64},{4,20},{8,72},{12,28},{16,80},{20,4},{24,88},{28,12},{32,96... | collective-permute-start | bytes 1425416 | tf_op jit(solution)/shard_map/ppermute | solution.py:203
  25.4 2.1 %collective-permute-start.7 = (bf16[1,256,896]{2,1,0:T(8,128)(2,1)}, bf16[1,256,896]{2,1,0:T(8,128)(2,1)}, u32[]{:S(2)}, u32[]{:S(2)}) collective-permute-start(bf16[1,256,896]{2,1,0:T(8,128)(2,1)} %get-tuple-element.52), channel_id=1, source_target_pairs={{0,2},{1,3},{2,0},{3,1},{4,6},{5,7},{6,4},{7,5},{8,10},{9,11},{10,... | collective-permute-start | bytes 1376264 | tf_op jit(solution)/shard_map/ppermute | solution.py:196
  31.5 2.3 %fusion.7 = (bf16[1024,640]{1,0:T(8,128)(2,1)}, bf16[1024,640]{1,0:T(8,128)(2,1)}) fusion(bf16[1024,576]{1,0:T(8,128)(2,1)S(1)} %reshape.127), kind=kLoop, calls=%fused_computation.32 | loop fusion | bytes 3801088 | tf_op jit(solution)/shard_map/jit(_pad)/pad | solution.py:364
  35.6 2.9 %collective-permute-done.7.refs_11_ = bf16[1,256,896]{2,1,0:T(8,128)(2,1)} collective-permute-done((bf16[1,256,896]{2,1,0:T(8,128)(2,1)}, bf16[1,256,896]{2,1,0:T(8,128)(2,1)}, u32[]{:S(2)}, u32[]{:S(2)}) %collective-permute-start.7) | collective-permute-done | bytes 458784 | tf_op jit(solution)/shard_map/ppermute | solution.py:196
  43.5 2.1 %collective-permute-start.12 = (bf16[2,256,896]{2,1,0:T(8,128)(2,1)}, bf16[2,256,896]{2,1,0:T(8,128)(2,1)}, u32[]{:S(2)}, u32[]{:S(2)}) collective-permute-start(bf16[2,256,896]{2,1,0:T(8,128)(2,1)} %get-tuple-element.57), channel_id=1, source_target_pairs={{0,3},{1,0},{2,1},{3,2},{4,7},{5,4},{6,5},{7,6},{8,11},{9,8},{10,9... | collective-permute-start | bytes 2752520 | tf_op jit(solution)/shard_map/ppermute | solution.py:196
  45.8 3.1 %fusion = bf16[4,8,288,128]{3,1,2,0:T(8,128)(2,1)S(1)} fusion(pred[32,64]{1,0:T(8,128)(4,1)S(1)} %and_reduce_fusion, bf16[64,36864]{1,0:T(8,128)(2,1)} %kv_ref.1), kind=kOutput, calls=%fused_computation.3 | convolution fusion | flops 152174592 | bytes 7079936 | tf_op jit(solution)/shard_map/dot_general | solution.py:401
  51.9 6.9 %shard_map.148.refs_6_ = bf16[2,128,256]{2,1,0:T(8,128)(2,1)} custom-call(s32[5]{0:T(128)} %stack.23.place_ref, bf16[256,3712]{1,0:T(8,128)(2,1)} %copy-done, bf16[256,3712]{1,0:T(8,128)(2,1)} %copy-done.3, bf16[2,3584,256]{2,1,0:T(8,128)(2,1)} %refs_4_.3, bf16[2,3584,256]{2,1,0:T(8,128)(2,1)} %refs_5_.3), custom_call_target="tpu_custom_call" | custom-call | flops 2000000000 | bytes 11500000 | tf_op jit(solution)/shard_map/pallas_call | solution.py:83
  58.9 6.9 %collective-permute-done.11.refs_9_ = bf16[2,256,896]{2,1,0:T(8,128)(2,1)} collective-permute-done((bf16[2,256,896]{2,1,0:T(8,128)(2,1)}, bf16[2,256,896]{2,1,0:T(8,128)(2,1)}, u32[]{:S(2)}, u32[]{:S(2)}) %collective-permute-start.11) | collective-permute-done | bytes 917536 | tf_op jit(solution)/shard_map/ppermute | solution.py:196
  69.5 2.7 %collective-permute-start.14 = (bf16[128,3712]{1,0:T(8,128)(2,1)}, bf16[128,3712]{1,0:T(8,128)(2,1)}, u32[]{:S(2)}, u32[]{:S(2)}) collective-permute-start(bf16[128,3712]{1,0:T(8,128)(2,1)} %slice.23), channel_id=1, source_target_pairs={{0,24},{4,100},{8,0},{12,108},{16,8},{20,116},{24,16},{28,124},{32... | collective-permute-start | bytes 2850824 | tf_op jit(solution)/shard_map/ppermute | solution.py:203
  76.5 10.0 %shard_map.149.refs_0_ = bf16[2,384,256]{2,1,0:T(8,128)(2,1)} custom-call(s32[5]{0:T(128)} %stack.23.place_ref, bf16[256,3712]{1,0:T(8,128)(2,1)} %copy-done.1, bf16[256,3712]{1,0:T(8,128)(2,1)} %copy-done.4, bf16[256,3712]{1,0:T(8,128)(2,1)} %copy-done.2, bf16[256,3712]{1,0:T(8,128)(2,1)} %copy-done.5, bf16[2,3584,256]{2,1,0:T(8,128)(2,1)} %refs_4_.3, ...), custom_call_target="tpu_custom_call" | custom-call | flops 4000000000 | bytes 15500000 | tf_op jit(solution)/shard_map/pallas_call | solution.py:83
  86.5 5.5 %all-to-all-start = ((bf16[32,288,128]{2,1,0:T(8,128)(2,1)}), bf16[32,288,128]{2,1,0:T(8,128)(2,1)S(1)}, u32[]{:S(2)}, u32[]{:S(2)}) async-start(bf16[32,288,128]{2,1,0:T(8,128)(2,1)} %bitcast.14), calls=%async_computation | async-start | bytes 4718592 | tf_op jit(solution)/shard_map/all_to_all | solution.py:271
  97.7 6.9 %shard_map.151.refs_4_ = bf16[2,128,256]{2,1,0:T(8,128)(2,1)} custom-call(s32[5]{0:T(128)} %stack.23.place_ref, bf16[128,3712]{1,0:T(8,128)(2,1)} %collective-permute-done.13.refs_0_, bf16[128,3712]{1,0:T(8,128)(2,1)} %collective-permute-done.14.refs_1_, bf16[128,3712]{1,0:T(8,128)(2,1)} %copy-done.7, bf16[128,3712]{1,0:T(8,128)(2,1)} %copy-done.8, ...), custom_call_target="tpu_custom_call" | custom-call | flops 2000000000 | bytes 11500000 | tf_op jit(solution)/shard_map/pallas_call | solution.py:83
  109.2 3.1 %collective-permute-done.20.refs_3_ = bf16[2,384,256]{2,1,0:T(8,128)(2,1)} collective-permute-done((bf16[2,384,256]{2,1,0:T(8,128)(2,1)S(1)}, bf16[2,384,256]{2,1,0:T(8,128)(2,1)}, u32[]{:S(2)}, u32[]{:S(2)}) %collective-permute-start.20) | collective-permute-done | bytes 393248 | tf_op jit(solution)/shard_map/ppermute | solution.py:196
  112.3 5.0 %collective-permute-done.23.refs_5_ = bf16[2,128,256]{2,1,0:T(8,128)(2,1)S(1)} collective-permute-done((bf16[2,128,256]{2,1,0:T(8,128)(2,1)}, bf16[2,128,256]{2,1,0:T(8,128)(2,1)S(1)}, u32[]{:S(2)}, u32[]{:S(2)}) %collective-permute-start.23) | collective-permute-done | bytes 131104 | tf_op jit(solution)/shard_map/ppermute | solution.py:196
  118.0 7.2 %shard_map.152 = bf16[128,8,896]{2,1,0:T(8,128)(2,1)} custom-call(s32[5]{0:T(128)} %stack.23.place_ref, bf16[2,384,256]{2,1,0:T(8,128)(2,1)} %shard_map.149.refs_0_, bf16[2,384,256]{2,1,0:T(8,128)(2,1)} %copy-done.14, bf16[2,384,256]{2,1,0:T(8,128)(2,1)} %collective-permute-done.19.refs_2_, bf16[2,384,256]{2,1,0:T(8,128)(2,1)} %collective-permute-done.20.refs_3_, ...), custom_call_target="tpu_custom_call" | custom-call | flops 3000000000 | bytes 8000000 | tf_op jit(solution)/shard_map/pallas_call | solution.py:138
  125.2 10.9 %all-to-all-start.1 = ((bf16[128,8,896]{2,1,0:T(8,128)(2,1)}), bf16[128,8,896]{2,1,0:T(8,128)(2,1)}, u32[]{:S(2)}, u32[]{:S(2)}) async-start(bf16[128,8,896]{2,1,0:T(8,128)(2,1)} %shard_map.152), calls=%async_computation.1 | async-start | bytes 3670016 | tf_op jit(solution)/shard_map/all_to_all | solution.py:277
  136.1 22.0 %shard_map.150 = bf16[1024,512]{1,0:T(8,128)(2,1)} custom-call(bf16[64,36864]{1,0:T(8,128)(2,1)} %kv_ref.1, bf16[1024,640]{1,0:T(8,128)(2,1)} %get-tuple-element.68.qe_ref, bf16[1024,640]{1,0:T(8,128)(2,1)} %get-tuple-element.69.qo_ref, bf16[128,640]{1,0:T(8,128)(2,1)} %pad.19.fresh_ref, s32[1,256]{1,0:T(1,128)} %reshape_tile.6.fill_ref, ...), custom_call_target="tpu_custom_call" | custom-call | flops 20000000000 | bytes 10000000 | tf_op jit(solution)/shard_map/pallas_call | solution.py:373
  158.1 2.6 %reshape.131 = bf16[2,4,65536]{2,1,0:T(4,128)(2,1)} reshape(bf16[1024,512]{1,0:T(8,128)(2,1)} %shard_map.150) | data formatting | bytes 2097152 | tf_op jit(solution)/shard_map/reshape | solution.py:392
  160.8 2.3 %copy.29 = bf16[4,8,288,128]{3,1,2,0:T(8,128)(2,1)} copy(bf16[4,8,288,128]{3,2,1,0:T(8,128)(2,1)S(1)} %bitcast.31) | data formatting | bytes 4718592
  164.0 2.5 %shard_map.153 = bf16[2,8,3584]{2,1,0:T(8,128)(2,1)} custom-call(f32[16,256]{1,0:T(8,128)} %copy.25.mix_ref, bf16[32,4,8,896]{3,2,1,0:T(8,128)(2,1)} %bitcast.11.ret_ref), custom_call_target="tpu_custom_call" | custom-call | tf_op jit(solution)/shard_map/pallas_call | solution.py:172
  (111 shorter events, 45.0 us)
Async XLA Ops:
  7.6 7.8 %collective-permute-start.1 = (bf16[16,3712]{1,0:T(8,128)(2,1)S(1)}, bf16[16,3712]{1,0:T(8,128)(2,1)S(1)}, u32[]{:S(2)}, u32[]{:S(2)}) collective-permute-start(bf16[16,3712]{1,0:T(8,128)(2,1)S(1)} %maximum_select_fusion), channel_id=1, source_target_pairs={{0,1},{1,2},{2,3},{3,0},{4,5},{5,6},{6,7},{7,4},{8,9},{9,10},{10,1... | collective-permute-start | bytes 356360 | tf_op jit(solution)/shard_map/ppermute | solution.py:196
  9.0 8.5 %collective-permute-start.2 = (bf16[16,3712]{1,0:T(8,128)(2,1)S(1)}, bf16[16,3712]{1,0:T(8,128)(2,1)S(1)}, u32[]{:S(2)}, u32[]{:S(2)}) collective-permute-start(bf16[16,3712]{1,0:T(8,128)(2,1)S(1)} %maximum_select_fusion), channel_id=1, source_target_pairs={{0,2},{1,3},{2,0},{3,1},{4,6},{5,7},{6,4},{7,5},{8,10},{9,11},{10,... | collective-permute-start | bytes 356360 | tf_op jit(solution)/shard_map/ppermute | solution.py:196
  17.6 16.2 %collective-permute-start.4 = (bf16[64,3712]{1,0:T(8,128)(2,1)S(1)}, bf16[64,3712]{1,0:T(8,128)(2,1)}, u32[]{:S(2)}, u32[]{:S(2)}) collective-permute-start(bf16[64,3712]{1,0:T(8,128)(2,1)S(1)} %pad_maximum_fusion.1), channel_id=1, source_target_pairs={{0,32},{4,12},{8,40},{12,20},{16,48},{20,28},{24,56},{28,4},{32,64... | collective-permute-start | bytes 1425416 | tf_op jit(solution)/shard_map/ppermute | solution.py:203
  19.3 14.8 %collective-permute-start.5 = (bf16[64,3712]{1,0:T(8,128)(2,1)S(1)}, bf16[64,3712]{1,0:T(8,128)(2,1)}, u32[]{:S(2)}, u32[]{:S(2)}) collective-permute-start(bf16[64,3712]{1,0:T(8,128)(2,1)S(1)} %pad_maximum_fusion.1), channel_id=1, source_target_pairs={{0,64},{4,20},{8,72},{12,28},{16,80},{20,4},{24,88},{28,12},{32,96... | collective-permute-start | bytes 1425416 | tf_op jit(solution)/shard_map/ppermute | solution.py:203
  22.6 11.5 %collective-permute-start.6 = (bf16[64,3712]{1,0:T(8,128)(2,1)S(1)}, bf16[64,3712]{1,0:T(8,128)(2,1)}, u32[]{:S(2)}, u32[]{:S(2)}) collective-permute-start(bf16[64,3712]{1,0:T(8,128)(2,1)S(1)} %pad_maximum_fusion.1), channel_id=1, source_target_pairs={{0,96},{4,28},{8,104},{12,4},{16,112},{20,12},{24,120},{28,20},{32... | collective-permute-start | bytes 1425416 | tf_op jit(solution)/shard_map/ppermute | solution.py:203
  25.4 13.1 %collective-permute-start.7 = (bf16[1,256,896]{2,1,0:T(8,128)(2,1)}, bf16[1,256,896]{2,1,0:T(8,128)(2,1)}, u32[]{:S(2)}, u32[]{:S(2)}) collective-permute-start(bf16[1,256,896]{2,1,0:T(8,128)(2,1)} %get-tuple-element.52), channel_id=1, source_target_pairs={{0,2},{1,3},{2,0},{3,1},{4,6},{5,7},{6,4},{7,5},{8,10},{9,11},{10,... | collective-permute-start | bytes 1376264 | tf_op jit(solution)/shard_map/ppermute | solution.py:196
  38.5 12.1 %collective-permute-start.10 = (bf16[256,3712]{1,0:T(8,128)(2,1)S(1)}, bf16[256,3712]{1,0:T(8,128)(2,1)S(1)}, u32[]{:S(2)}, u32[]{:S(2)}) collective-permute-start(bf16[256,3712]{1,0:T(8,128)(2,1)S(1)} %pad_maximum_fusion.refs_0_), channel_id=1, source_target_pairs={{0,4},{4,0},{8,12},{12,8},{16,20},{20,16},{24,28},{28,24},{32,36},... | collective-permute-start | bytes 5701640 | tf_op jit(solution)/shard_map/ppermute | solution.py:203
  40.2 25.6 %collective-permute-start.8 = (bf16[256,3712]{1,0:T(8,128)(2,1)S(1)}, bf16[256,3712]{1,0:T(8,128)(2,1)S(1)}, u32[]{:S(2)}, u32[]{:S(2)}) collective-permute-start(bf16[256,3712]{1,0:T(8,128)(2,1)S(1)} %pad_maximum_fusion.refs_0_), channel_id=1, source_target_pairs={{0,8},{4,36},{8,16},{12,44},{16,24},{20,52},{24,0},{28,60},{32,40}... | collective-permute-start | bytes 5701640 | tf_op jit(solution)/shard_map/ppermute | solution.py:203
  41.5 24.4 %collective-permute-start.9 = (bf16[256,3712]{1,0:T(8,128)(2,1)S(1)}, bf16[256,3712]{1,0:T(8,128)(2,1)S(1)}, u32[]{:S(2)}, u32[]{:S(2)}) collective-permute-start(bf16[256,3712]{1,0:T(8,128)(2,1)S(1)} %pad_maximum_fusion.refs_0_), channel_id=1, source_target_pairs={{0,24},{4,100},{8,0},{12,108},{16,8},{20,116},{24,16},{28,124},{32... | collective-permute-start | bytes 5701640 | tf_op jit(solution)/shard_map/ppermute | solution.py:203
  42.9 22.9 %collective-permute-start.11 = (bf16[2,256,896]{2,1,0:T(8,128)(2,1)}, bf16[2,256,896]{2,1,0:T(8,128)(2,1)}, u32[]{:S(2)}, u32[]{:S(2)}) collective-permute-start(bf16[2,256,896]{2,1,0:T(8,128)(2,1)} %get-tuple-element.56), channel_id=1, source_target_pairs={{0,1},{1,2},{2,3},{3,0},{4,5},{5,6},{6,7},{7,4},{8,9},{9,10},{10,1... | collective-permute-start | bytes 2752520 | tf_op jit(solution)/shard_map/ppermute | solution.py:196
  43.5 22.3 %collective-permute-start.12 = (bf16[2,256,896]{2,1,0:T(8,128)(2,1)}, bf16[2,256,896]{2,1,0:T(8,128)(2,1)}, u32[]{:S(2)}, u32[]{:S(2)}) collective-permute-start(bf16[2,256,896]{2,1,0:T(8,128)(2,1)} %get-tuple-element.57), channel_id=1, source_target_pairs={{0,3},{1,0},{2,1},{3,2},{4,7},{5,4},{6,5},{7,6},{8,11},{9,8},{10,9... | collective-permute-start | bytes 2752520 | tf_op jit(solution)/shard_map/ppermute | solution.py:196
  65.8 8.2 %collective-permute-start.15 = (bf16[256,3712]{1,0:T(8,128)(2,1)S(1)}, bf16[256,3712]{1,0:T(8,128)(2,1)S(1)}, u32[]{:S(2)}, u32[]{:S(2)}) collective-permute-start(bf16[256,3712]{1,0:T(8,128)(2,1)S(1)} %collective-permute-done.8.refs_0_), channel_id=1, source_target_pairs={{0,4},{4,0},{8,12},{12,8},{16,20},{20,16},{24,28},{28,24},{32,36},... | collective-permute-start | bytes 5701640 | tf_op jit(solution)/shard_map/ppermute | solution.py:203
  67.3 6.7 %collective-permute-start.16 = (bf16[256,3712]{1,0:T(8,128)(2,1)S(1)}, bf16[256,3712]{1,0:T(8,128)(2,1)S(1)}, u32[]{:S(2)}, u32[]{:S(2)}) collective-permute-start(bf16[256,3712]{1,0:T(8,128)(2,1)S(1)} %collective-permute-done.9.refs_2_), channel_id=1, source_target_pairs={{0,4},{4,0},{8,12},{12,8},{16,20},{20,16},{24,28},{28,24},{32,36},... | collective-permute-start | bytes 5701640 | tf_op jit(solution)/shard_map/ppermute | solution.py:203
  69.5 17.0 %collective-permute-start.13 = (bf16[128,3712]{1,0:T(8,128)(2,1)}, bf16[128,3712]{1,0:T(8,128)(2,1)}, u32[]{:S(2)}, u32[]{:S(2)}) collective-permute-start(bf16[128,3712]{1,0:T(8,128)(2,1)} %slice.22), channel_id=1, source_target_pairs={{0,8},{4,36},{8,16},{12,44},{16,24},{20,52},{24,0},{28,60},{32,40}... | collective-permute-start | bytes 2850824 | tf_op jit(solution)/shard_map/ppermute | solution.py:203
  69.5 17.0 %collective-permute-start.14 = (bf16[128,3712]{1,0:T(8,128)(2,1)}, bf16[128,3712]{1,0:T(8,128)(2,1)}, u32[]{:S(2)}, u32[]{:S(2)}) collective-permute-start(bf16[128,3712]{1,0:T(8,128)(2,1)} %slice.23), channel_id=1, source_target_pairs={{0,24},{4,100},{8,0},{12,108},{16,8},{20,116},{24,16},{28,124},{32... | collective-permute-start | bytes 2850824 | tf_op jit(solution)/shard_map/ppermute | solution.py:203
  72.2 14.3 %collective-permute-start.17 = (bf16[1,256,896]{2,1,0:T(8,128)(2,1)S(1)}, bf16[1,256,896]{2,1,0:T(8,128)(2,1)}, u32[]{:S(2)}, u32[]{:S(2)}) collective-permute-start(bf16[1,256,896]{2,1,0:T(8,128)(2,1)S(1)} %get-tuple-element.65), channel_id=1, source_target_pairs={{0,2},{1,3},{2,0},{3,1},{4,6},{5,7},{6,4},{7,5},{8,10},{9,11},{10,... | collective-permute-start | bytes 1376264 | tf_op jit(solution)/shard_map/ppermute | solution.py:196
  86.5 38.7 %all-to-all-start = ((bf16[32,288,128]{2,1,0:T(8,128)(2,1)}), bf16[32,288,128]{2,1,0:T(8,128)(2,1)S(1)}, u32[]{:S(2)}, u32[]{:S(2)}) async-start(bf16[32,288,128]{2,1,0:T(8,128)(2,1)} %bitcast.14), calls=%async_computation | async-start | bytes 4718592 | tf_op jit(solution)/shard_map/all_to_all | solution.py:271
  92.6 14.7 %collective-permute-start.18 = (bf16[2,384,256]{2,1,0:T(8,128)(2,1)S(1)}, bf16[2,384,256]{2,1,0:T(8,128)(2,1)S(1)}, u32[]{:S(2)}, u32[]{:S(2)}) collective-permute-start(bf16[2,384,256]{2,1,0:T(8,128)(2,1)S(1)} %copy-done.9), channel_id=1, source_target_pairs={{0,1},{1,2},{2,3},{3,0},{4,5},{5,6},{6,7},{7,4},{8,9},{9,10},{10,1... | collective-permute-start | bytes 1179656 | tf_op jit(solution)/shard_map/ppermute | solution.py:196
  94.1 15.2 %collective-permute-start.19 = (bf16[2,384,256]{2,1,0:T(8,128)(2,1)S(1)}, bf16[2,384,256]{2,1,0:T(8,128)(2,1)}, u32[]{:S(2)}, u32[]{:S(2)}) collective-permute-start(bf16[2,384,256]{2,1,0:T(8,128)(2,1)S(1)} %copy-done.9), channel_id=1, source_target_pairs={{0,3},{1,0},{2,1},{3,2},{4,7},{5,4},{6,5},{7,6},{8,11},{9,8},{10,9... | collective-permute-start | bytes 1179656 | tf_op jit(solution)/shard_map/ppermute | solution.py:196
  95.3 17.0 %collective-permute-start.20 = (bf16[2,384,256]{2,1,0:T(8,128)(2,1)S(1)}, bf16[2,384,256]{2,1,0:T(8,128)(2,1)}, u32[]{:S(2)}, u32[]{:S(2)}) collective-permute-start(bf16[2,384,256]{2,1,0:T(8,128)(2,1)S(1)} %copy-done.9), channel_id=1, source_target_pairs={{0,2},{1,3},{2,0},{3,1},{4,6},{5,7},{6,4},{7,5},{8,10},{9,11},{10,... | collective-permute-start | bytes 1179656 | tf_op jit(solution)/shard_map/ppermute | solution.py:196
  104.7 12.7 %collective-permute-start.23 = (bf16[2,128,256]{2,1,0:T(8,128)(2,1)}, bf16[2,128,256]{2,1,0:T(8,128)(2,1)S(1)}, u32[]{:S(2)}, u32[]{:S(2)}) collective-permute-start(bf16[2,128,256]{2,1,0:T(8,128)(2,1)} %shard_map.151.refs_4_), channel_id=1, source_target_pairs={{0,1},{1,2},{2,3},{3,0},{4,5},{5,6},{6,7},{7,4},{8,9},{9,10},{10,1... | collective-permute-start | bytes 393224 | tf_op jit(solution)/shard_map/ppermute | solution.py:196
  105.5 11.8 %collective-permute-start.24 = (bf16[2,128,256]{2,1,0:T(8,128)(2,1)}, bf16[2,128,256]{2,1,0:T(8,128)(2,1)}, u32[]{:S(2)}, u32[]{:S(2)}) collective-permute-start(bf16[2,128,256]{2,1,0:T(8,128)(2,1)} %shard_map.151.refs_4_), channel_id=1, source_target_pairs={{0,3},{1,0},{2,1},{3,2},{4,7},{5,4},{6,5},{7,6},{8,11},{9,8},{10,9... | collective-permute-start | bytes 393224 | tf_op jit(solution)/shard_map/ppermute | solution.py:196
  107.3 10.0 %collective-permute-start.25 = (bf16[2,128,256]{2,1,0:T(8,128)(2,1)}, bf16[2,128,256]{2,1,0:T(8,128)(2,1)}, u32[]{:S(2)}, u32[]{:S(2)}) collective-permute-start(bf16[2,128,256]{2,1,0:T(8,128)(2,1)} %shard_map.151.refs_4_), channel_id=1, source_target_pairs={{0,2},{1,3},{2,0},{3,1},{4,6},{5,7},{6,4},{7,5},{8,10},{9,11},{10,... | collective-permute-start | bytes 393224 | tf_op jit(solution)/shard_map/ppermute | solution.py:196
  125.2 38.8 %all-to-all-start.1 = ((bf16[128,8,896]{2,1,0:T(8,128)(2,1)}), bf16[128,8,896]{2,1,0:T(8,128)(2,1)}, u32[]{:S(2)}, u32[]{:S(2)}) async-start(bf16[128,8,896]{2,1,0:T(8,128)(2,1)} %shard_map.152), calls=%async_computation.1 | async-start | bytes 3670016 | tf_op jit(solution)/shard_map/all_to_all | solution.py:277
  (20 other events, 142.5 us)
